TPU v7x, 32 devices: a whole 2x2x4 slice. The times are simulated.
32 devices in a mesh: seq: 8 (over z, y), head: 4 (over x, core).
Axes of the slice: x: 2, y: 2, z: 4, core: 2. Of those that a mesh axis runs over, the one named last changes fastest.
Arguments:
- queries: bfloat16 [1, 4096, 1024], P(None, 'seq', 'head'), may hold values from -40 to 40
- key_vectors: bfloat16 [1, 4096, 1024], P(None, 'seq', 'head'), may hold values from -40 to 40
- value_vectors: bfloat16 [1, 4096, 1024], P(None, 'seq', 'head'), may hold values from -6 to 6
- out_weight: bfloat16 [1024, 1024], replicated, may hold values from -0.1875 to 0.1875
Outputs:
- layer_output: bfloat16 [1, 4096, 1024], P(None, ('seq', 'head'))
All inputs are finite; a program needn't handle non-finite values.
Results may differ from a plain program's by a relative error of at most 0.038.
Values may be sent and summed in bfloat16 or wider, within the bound.
No kernel may reach another device: no remote copies, remote signals or barrier semaphores. Data moves between devices by JAX's collectives and lax.ppermute only.
A program may use at most 192 MiB of HBM per device.

v0:
```python
import jax
import jax.numpy as jnp
from jax import lax
from jax.experimental import pallas as pl
from jax.experimental.pallas import tpu as pltpu
from jax.sharding import PartitionSpec as P

HD = 64
BLOCK = 128
LEVELS = 4
SLAB = 8
PAIR = 2 * HD

neg_fill = -1e30
root_half = 0.7071067811865476
log2_scale = HD**-0.5 * 1.4426950408889634

FAN = 2**LEVELS


def slabs_of(scratch, block):
    return [scratch[pl.ds(BLOCK * block + j, SLAB, stride=FAN), :] for j in range(FAN)]


def pooled_slabs(slabs):
    return [
        ((low + high) * root_half).astype(jnp.bfloat16).astype(jnp.float32)
        for low, high in zip(slabs[0::2], slabs[1::2])
    ]


def joined(slabs):
    return jnp.concatenate(slabs, axis=0).astype(jnp.bfloat16)


def spill(source, scratch):
    for half in range(scratch.shape[0]):
        scratch[half] = source[:, half * PAIR : (half + 1) * PAIR].astype(jnp.float32)


def pool_kernel(
    k_hbm, v_hbm, q_hbm, k_ref, v_ref, q_ref, first_ref, one_ref, two_ref, scratch, sems, q_sem
):
    rows = k_ref.shape[0]
    blocks = rows // BLOCK
    arrivals = []
    for block in range(blocks):
        here = pl.ds(block * BLOCK, BLOCK)
        for which, (source, target) in enumerate(((k_hbm, k_ref), (v_hbm, v_ref))):
            copy = pltpu.make_async_copy(
                source.at[0, here, :], target.at[here, :], sems.at[which, block]
            )
            copy.start()
            arrivals.append((block, which, target, copy))
    q_copy = pltpu.make_async_copy(q_hbm.at[0], q_ref, q_sem.at[0])
    q_copy.start()
    even = lax.rem(lax.axis_index("seq"), 2) == 0
    for block, which, ref, copy in arrivals:
        copy.wait()
        here = pl.ds(block * BLOCK, BLOCK)
        spill(ref.at[here, :], scratch.at[which, block])
        for half in range(scratch.shape[2]):
            lanes = pl.ds(half * PAIR, PAIR)
            one = pooled_slabs(slabs_of(scratch.at[which, block, half], 0))
            one_ref[which, pl.ds(block * BLOCK // 2, BLOCK // 2), lanes] = joined(one)
            two_ref[which, pl.ds(block * BLOCK // 4, BLOCK // 4), lanes] = joined(pooled_slabs(one))
    inner = rows // 4 - BLOCK // 4
    for which, ref in enumerate((k_ref, v_ref)):
        first_ref[which, :BLOCK, :] = jnp.where(even, ref[rows - BLOCK :, :], ref[:BLOCK, :])
        first_ref[which, BLOCK:, :] = jnp.where(
            even, two_ref[which, :inner, :], two_ref[which, BLOCK // 4 :, :]
        )
    q_copy.wait()


def repooled(field):
    rows, lanes = field.shape
    slabs = field.astype(jnp.float32).reshape(rows // (2 * SLAB), 2, SLAB, lanes)
    return ((slabs[:, 0] + slabs[:, 1]) * root_half).reshape(rows // 2, lanes).astype(jnp.bfloat16)


def deeper_kernel(k_ref, v_ref, two_ref, second_ref, three_ref, four_ref):
    rows = k_ref.shape[0]
    even = lax.rem(lax.axis_index("seq"), 2) == 0
    for which, ref in enumerate((k_ref, v_ref)):
        second_ref[which] = jnp.where(even, ref[:BLOCK, :], ref[rows - BLOCK :, :])
        three = repooled(two_ref[which])
        three_ref[which] = three
        four_ref[which] = repooled(three)


def repooled(field):
    rows, lanes = field.shape
    slabs = field.astype(jnp.float32).reshape(rows // (2 * SLAB), 2, SLAB, lanes)
    return ((slabs[:, 0] + slabs[:, 1]) * root_half).reshape(rows // 2, lanes).astype(jnp.bfloat16)


def score(queries, keys, hold, is_open=None):
    rows = queries.shape[0]
    low = lax.broadcasted_iota(jnp.int32, (rows, PAIR), 1) < HD
    zero = jnp.zeros_like(queries)
    both = jnp.concatenate([jnp.where(low, queries, zero), jnp.where(low, zero, queries)], axis=0)
    raw = lax.dot_general(both, keys, (((1,), (1,)), ((), ())), preferred_element_type=jnp.float32)
    if is_open is not None:
        raw = jnp.where(is_open, raw, neg_fill)
    hold[...] = raw
    return jnp.max(raw, axis=1, keepdims=True)


def weigh(hold, top, values):
    rows = top.shape[0] // 2
    low = lax.broadcasted_iota(jnp.int32, (rows, PAIR), 1) < HD
    weights = jnp.exp2((hold[...] - top) * log2_scale).astype(jnp.bfloat16)
    result = jnp.dot(weights, values, preferred_element_type=jnp.float32)
    return (
        log2_scale * jnp.where(low, top[:rows], top[rows:]),
        jnp.where(low, result[:rows, :PAIR], result[rows:, :PAIR]),
        jnp.where(low, result[:rows, PAIR:], result[rows:, PAIR:]),
    )


def merged(fine, coarse):
    top = jnp.maximum(fine[0], coarse[0])
    keep = jnp.exp2(fine[0] - top)
    join = jnp.exp2(coarse[0] - top)
    return top, fine[1] * keep + coarse[1] * join, fine[2] * keep + coarse[2] * join


def doubled(field):
    rows, lanes = field.shape
    slabs = field.reshape(rows // SLAB, 1, SLAB, lanes)
    return jnp.broadcast_to(slabs, (rows // SLAB, 2, SLAB, lanes)).reshape(2 * rows, lanes)


def with_ones(values, weight=1.0):
    if weight != 1.0:
        values = values * jnp.bfloat16(weight)
    return jnp.concatenate([values, jnp.full(values.shape, weight, jnp.bfloat16)], axis=1)


def local_kernel(
    q_ref, k_ref, v_ref, one_ref, edge_q, two_q, three_q, four_q, state,
    scratch, near_hold, coarse_hold,
):
    rows = q_ref.shape[0]
    blocks = rows // BLOCK
    pairs = scratch.shape[0]
    spill(q_ref, scratch)
    fine, one_q = [], []
    for pair in range(pairs):
        lanes = pl.ds(pair * PAIR, PAIR)
        ladder = [[], [], [], [], []]
        for block in range(blocks):
            slabs = slabs_of(scratch.at[pair], block)
            ladder[0].append(joined(slabs))
            for level in range(1, LEVELS + 1):
                slabs = pooled_slabs(slabs)
                ladder[level] += slabs
        edge_q[0, :, lanes] = ladder[0][0]
        edge_q[1, :, lanes] = ladder[0][-1]
        two_q[:, lanes] = joined(ladder[2])
        three_q[:, lanes] = joined(ladder[3])
        four_q[:, lanes] = joined(ladder[4])
        fine.append(ladder[0])
        one_q.append([joined(ladder[1][n : n + FAN]) for n in range(0, len(ladder[1]), FAN)])
    windows = [(max(n - 1, 0) * BLOCK, min(n + 2, blocks) * BLOCK) for n in range(blocks)]
    tops = {}
    for pair in range(pairs):
        lanes = pl.ds(pair * PAIR, PAIR)
        for half in range(blocks // 2):
            there = pl.ds((half ^ 1) * BLOCK, BLOCK)
            tops[pair, half] = score(
                one_q[pair][half], one_ref[0, there, lanes], coarse_hold.at[pair, half]
            )
            for block in (2 * half, 2 * half + 1):
                low, high = windows[block]
                hold = near_hold.at[pair, block, :, : high - low]
                tops[pair, half, block] = score(fine[pair][block], k_ref[low:high, lanes], hold)
    for pair in range(pairs):
        lanes = pl.ds(pair * PAIR, PAIR)
        for half in range(blocks // 2):
            there = pl.ds((half ^ 1) * BLOCK, BLOCK)
            coarse = weigh(
                coarse_hold.at[pair, half], tops[pair, half], with_ones(one_ref[1, there, lanes])
            )
            for block in (2 * half, 2 * half + 1):
                low, high = windows[block]
                hold = near_hold.at[pair, block, :, : high - low]
                near = weigh(hold, tops[pair, half, block], with_ones(v_ref[low:high, lanes]))
                part = slice((block - 2 * half) * BLOCK // 2, (block - 2 * half + 1) * BLOCK // 2)
                done = merged(near, [doubled(x[part]) for x in coarse])
                for index, field in enumerate(done):
                    state[index, block * BLOCK : (block + 1) * BLOCK, lanes] = field


def relay_kernel(first_ref, six_ref, four_ref, pack_ref, two_ref, near_ref, scratch):
    sixteenth = four_ref.shape[1]
    pack_ref[:, :sixteenth, :] = six_ref[...]
    pack_ref[:, sixteenth:, :] = four_ref[...]
    inner = first_ref.shape[1] - BLOCK
    two_ref[:, :inner, :] = first_ref[:, BLOCK:, :]
    for which in range(2):
        spill(first_ref.at[which, pl.ds(0, BLOCK), :], scratch.at[which])
        for half in range(scratch.shape[1]):
            lanes = pl.ds(half * PAIR, PAIR)
            slabs = slabs_of(scratch.at[which, half], 0)
            two_ref[which, inner:, lanes] = joined(pooled_slabs(pooled_slabs(slabs)))
        near_ref[which] = repooled(repooled(two_ref[which]))


def join_kernel(pack_ref, three_ref, relay_ref):
    eighth = three_ref.shape[1]
    relay_ref[:, :eighth, :] = three_ref[...]
    relay_ref[:, eighth:, :] = pack_ref[...]


def mid_kernel(edge_q, two_q, state, first_ref, second_ref, two_ref, out, holds):
    rows = state.shape[1]
    blocks = rows // BLOCK
    position = lax.axis_index("seq")
    last = lax.axis_size("seq") - 1
    even = lax.rem(position, 2) == 0
    opens = (position > 0, position < last)
    pairs = two_q.shape[1] // PAIR
    steps = {}
    for pair in range(pairs):
        lanes = pl.ds(pair * PAIR, PAIR)
        inner = [first_ref[which, :BLOCK, lanes] for which in range(2)]
        outer = [second_ref[which, :, lanes] for which in range(2)]
        steps[pair, 2] = (
            score(two_q[:, lanes], two_ref[0, :, lanes], holds.at[pair, 2]),
            with_ones(two_ref[1, :, lanes]),
        )
        for side in range(2):
            halo = [
                jnp.where(even, *((outer[which], inner[which])[:: 1 - 2 * side]))
                for which in range(2)
            ]
            steps[pair, side] = (
                score(edge_q[side, :, lanes], halo[0], holds.at[pair, side], opens[side]),
                with_ones(halo[1]),
            )
    for pair in range(pairs):
        lanes = pl.ds(pair * PAIR, PAIR)
        two = weigh(holds.at[pair, 2], *steps[pair, 2])
        for block in range(blocks):
            here = slice(block * BLOCK, (block + 1) * BLOCK)
            quarter = slice(block * BLOCK // 4, (block + 1) * BLOCK // 4)
            done = merged(
                [state[index, here, lanes] for index in range(3)],
                [doubled(doubled(x[quarter])) for x in two],
            )
            for side, edge in enumerate((0, blocks - 1)):
                if block == edge:
                    done = merged(done, weigh(holds.at[pair, side], *steps[pair, side]))
            for index, field in enumerate(done):
                out[index, here, lanes] = field


def finish_kernel(three_q, four_q, state, four_ref, near_ref, relay_a, relay_b, *refs):
    far, refs = refs[:-7], refs[-7:]
    outs, (attended, three_hold, four_hold) = refs[:-3], refs[-3:]
    rows = state.shape[1]
    blocks = rows // BLOCK
    own = lax.axis_index("head")
    pairs = three_q.shape[1] // PAIR
    eighth = rows // 8
    steps = {}
    for pair in range(pairs):
        lanes = pl.ds(pair * PAIR, PAIR)
        relays = [relay_a[:, :, lanes], relay_b[:, :, lanes]]
        three, ours, theirs, beyond = [], [], [], []
        for which in range(2):
            three.append([relay[which, :eighth] for relay in relays])
            ours.append(
                [four_ref[which, :, lanes], near_ref[which, :, lanes]]
                + [repooled(field) for field in three[which]]
            )
            theirs.append([relay[which, eighth:] for relay in relays])
            beyond.append([field[which, :, lanes] for field in far])
        steps[pair, 3] = (
            score(three_q[:, lanes], jnp.concatenate(three[0], axis=0), three_hold.at[pair]),
            with_ones(jnp.concatenate(three[1], axis=0)),
        )
        steps[pair, 4] = (
            score(
                four_q[:, lanes],
                jnp.concatenate(ours[0] + theirs[0] + beyond[0], axis=0),
                four_hold.at[pair],
            ),
            jnp.concatenate(
                [with_ones(field) for field in ours[1]]
                + [with_ones(field, 2.0) for field in theirs[1]]
                + [with_ones(field) for field in beyond[1]],
                axis=0,
            ),
        )
    for pair in range(pairs):
        lanes = pl.ds(pair * PAIR, PAIR)
        four = weigh(four_hold.at[pair], *steps[pair, 4])
        now = merged(weigh(three_hold.at[pair], *steps[pair, 3]), [doubled(x) for x in four])
        for block in range(blocks):
            here = slice(block * BLOCK, (block + 1) * BLOCK)
            eighth_here = slice(block * BLOCK // 8, (block + 1) * BLOCK // 8)
            _, numer, rowsum = merged(
                [state[index, here, lanes] for index in range(3)],
                [doubled(doubled(doubled(x[eighth_here]))) for x in now],
            )
            attended[block, :, lanes] = (numer / rowsum).astype(jnp.bfloat16)
    for step, out in enumerate(outs):
        out[...] = attended[own ^ step]


def partial_kernel(near_ref, next_ref, weight_ref, out_ref):
    own = lax.axis_index("head")
    features = near_ref.shape[1]
    total = None
    for step, part in enumerate((near_ref, next_ref)):
        start = pl.multiple_of((own ^ step) * features, features)
        product = jnp.dot(
            part[...], weight_ref[pl.ds(start, features), :], preferred_element_type=jnp.float32
        )
        total = product if total is None else total + product
    out_ref[...] = total


def project_kernel(partial_ref, *refs):
    parts, (weight_ref, out_hbm, scratch, staged, sems) = refs[:-5], refs[-5:]
    own = lax.axis_index("head")
    features = parts[0].shape[1]
    chunk = staged.shape[2]
    copies = []
    for index in range(staged.shape[0]):
        columns = pl.ds(index * chunk, chunk)
        total = partial_ref[:, columns]
        for step, part in enumerate(parts, 2):
            start = pl.multiple_of((own ^ step) * features, features)
            total += jnp.dot(
                part[...],
                weight_ref[pl.ds(start, features), columns],
                preferred_element_type=jnp.float32,
            )
        for half in range(chunk // PAIR):
            lanes = slice(half * PAIR, (half + 1) * PAIR)
            scratch[index, half] = total[:, lanes]
            for i in range(SLAB):
                staged[index, i * FAN : (i + 1) * FAN, lanes] = scratch[
                    index, half, pl.ds(i, FAN, stride=SLAB), :
                ].astype(jnp.bfloat16)
        copy = pltpu.make_async_copy(staged.at[index], out_hbm.at[:, columns], sems.at[index])
        copy.start()
        copies.append(copy)
    for copy in copies:
        copy.wait()


def repool_outside(field):
    which, rows, lanes = field.shape
    slabs = field.astype(jnp.float32).reshape(which, rows // (2 * SLAB), 2, SLAB, lanes)
    sums = (slabs[:, :, 0] + slabs[:, :, 1]) * root_half
    return sums.reshape(which, rows // 2, lanes).astype(jnp.bfloat16)


def swapped(block, axis, mask):
    return lax.ppermute(block, axis, [(i, i ^ mask) for i in range(lax.axis_size(axis))])


def across(block, axis):
    count = lax.axis_size(axis)
    route = []
    for low in range(1, count - 1, 2):
        route += [(low, low + 1), (low + 1, low)]
    return lax.ppermute(block, axis, route)


def per_device(queries, key_vectors, value_vectors, out_weight):
    rows, features = queries.shape[1:]
    queries, key_vectors, value_vectors = [
        pltpu.with_memory_space_constraint(x, pltpu.HBM)
        for x in (queries, key_vectors, value_vectors)
    ]
    pairs = features // PAIR
    seq_count, head_count = lax.axis_size("seq"), lax.axis_size("head")
    bf16 = lambda *shape: jax.ShapeDtypeStruct(shape, jnp.bfloat16)
    params = pltpu.CompilerParams(vmem_limit_bytes=32 * 1024 * 1024)

    hbm = pl.BlockSpec(memory_space=pltpu.HBM)
    vmem = pl.BlockSpec(memory_space=pltpu.VMEM)
    keys, values, ours, first, one, two = pl.pallas_call(
        pool_kernel,
        in_specs=[hbm] * 3,
        out_shape=[
            bf16(rows, features),
            bf16(rows, features),
            bf16(rows, features),
            bf16(2, BLOCK + rows // 4 - BLOCK // 4, features),
            bf16(2, rows // 2, features),
            bf16(2, rows // 4, features),
        ],
        scratch_shapes=[
            pltpu.VMEM((2, rows // BLOCK, pairs, BLOCK, PAIR), jnp.float32),
            pltpu.SemaphoreType.DMA((2, rows // BLOCK)),
            pltpu.SemaphoreType.DMA((1,)),
        ],
        compiler_params=params,
        name="pool",
    )(key_vectors, value_vectors, queries)
    second, three, four = pl.pallas_call(
        deeper_kernel,
        out_shape=[
            bf16(2, BLOCK, features),
            bf16(2, rows // 8, features),
            bf16(2, rows // 16, features),
        ],
        compiler_params=params,
        cost_estimate=pl.CostEstimate(flops=2**31, bytes_accessed=2**23, transcendentals=0),
        name="deeper",
    )(keys, values, two)

    first_in = swapped(first, "seq", 1)
    second_in = across(second, "seq")
    fours_in = [swapped(four, "seq", mask) for mask in (6, 4)]
    three_in = swapped(three, "seq", 2)
    pack, two_in, near = pl.pallas_call(
        relay_kernel,
        out_shape=[
            bf16(2, rows // 8, features),
            bf16(2, rows // 4, features),
            bf16(2, rows // 16, features),
        ],
        scratch_shapes=[pltpu.VMEM((2, pairs, BLOCK, PAIR), jnp.float32)],
        compiler_params=params,
        cost_estimate=pl.CostEstimate(flops=2**29, bytes_accessed=2**20, transcendentals=0),
        name="relay",
    )(first_in, *fours_in)
    relayed = pl.pallas_call(
        join_kernel,
        out_shape=bf16(2, rows // 4, features),
        compiler_params=params,
        name="join",
    )(pack, three_in)
    relayed_in = swapped(relayed, "seq", 1)

    edge_q, two_q, three_q, four_q, state = pl.pallas_call(
        local_kernel,
        out_shape=[
            bf16(2, BLOCK, features),
            bf16(rows // 4, features),
            bf16(rows // 8, features),
            bf16(rows // 16, features),
            jax.ShapeDtypeStruct((3, rows, features), jnp.float32),
        ],
        scratch_shapes=[
            pltpu.VMEM((pairs, rows, PAIR), jnp.float32),
            pltpu.VMEM((pairs, rows // BLOCK, 2 * BLOCK, 3 * BLOCK), jnp.float32),
            pltpu.VMEM((pairs, rows // BLOCK // 2, 2 * BLOCK, BLOCK), jnp.float32),
        ],
        compiler_params=params,
        name="local",
    )(ours, keys, values, one)

    state = pl.pallas_call(
        mid_kernel,
        out_shape=jax.ShapeDtypeStruct((3, rows, features), jnp.float32),
        input_output_aliases={2: 0},
        scratch_shapes=[pltpu.VMEM((pairs, 3, 2 * BLOCK, BLOCK), jnp.float32)],
        compiler_params=params,
        name="mid",
    )(edge_q, two_q, state, first_in, second_in, two_in)

    far = []
    known = 8
    if known < seq_count:
        eighth = rows // 8
        group = [four, near, repool_outside(relayed[:, :eighth]), repool_outside(relayed_in[:, :eighth])]
        group = jnp.concatenate(group + [relayed[:, eighth:], relayed_in[:, eighth:]], axis=1)
        while known < seq_count:
            fresh = swapped(group, "seq", known)
            far.append(fresh)
            group = jnp.concatenate([group, fresh], axis=1)
            known *= 2

    outs = pl.pallas_call(
        finish_kernel,
        out_shape=[bf16(BLOCK, features) for _ in range(head_count)],
        scratch_shapes=[
            pltpu.VMEM((rows // BLOCK, BLOCK, features), jnp.bfloat16),
            pltpu.VMEM((pairs, rows // 4, BLOCK), jnp.float32),
            pltpu.VMEM((pairs, rows // 8, rows // 16 * seq_count), jnp.float32),
        ],
        compiler_params=params,
        name="finish",
    )(three_q, four_q, state, four, near, relayed, relayed_in, *far)

    parts = [part if step == 0 else swapped(part, "head", step) for step, part in enumerate(outs)]
    width = out_weight.shape[1]
    partial = pl.pallas_call(
        partial_kernel,
        out_shape=jax.ShapeDtypeStruct((BLOCK, width), jnp.float32),
        compiler_params=params,
        name="partial",
    )(*parts[:2], out_weight)
    chunk = 2 * PAIR
    result = pl.pallas_call(
        project_kernel,
        in_specs=[vmem] * len(parts),
        out_specs=hbm,
        out_shape=bf16(BLOCK, width),
        scratch_shapes=[
            pltpu.VMEM((width // chunk, 2, BLOCK, PAIR), jnp.float32),
            pltpu.VMEM((width // chunk, BLOCK, chunk), jnp.bfloat16),
            pltpu.SemaphoreType.DMA((width // chunk,)),
        ],
        compiler_params=params,
        name="project",
    )(partial, *parts[2:], out_weight)
    return result[None]


def solution(mesh):
    return jax.shard_map(
        per_device,
        mesh=mesh,
        in_specs=(P(None, "seq", "head"), P(None, "seq", "head"), P(None, "seq", "head"), P()),
        out_specs=P(None, ("seq", "head"), None),
        check_vma=False,
    )
```

profile of v0, /device:TPU:0, one launch (start us, length us, event | category | flops | bytes accessed | tf_op | source)
XLA Modules:
  0.0 25.6 jit_solution(1681982214994023980)
XLA Ops:
  0.0 1.4 %pool.1 = (bf16[512,256]{1,0:T(8,128)(2,1)S(1)}, bf16[512,256]{1,0:T(8,128)(2,1)S(1)}, bf16[512,256]{1,0:T(8,128)(2,1)S(1)}, bf16[2,224,256]{2,1,0:T(8,128)(2,1)...) custom-call(bf16[1,512,256]{2,1,0:T(8,128)(2,1)} %k_hbm.1, bf16[1,512,256]{2,1,0:T(8,128)(2,1)} %v_hbm.1, ...), custom_call_target="tpu_custom_call" | custom-call | tf_op jit(solution)/shard_map/pool/pallas_call | solution.py:389
  1.4 3.0 %collective-permute-start = (bf16[2,224,256]{2,1,0:T(8,128)(2,1)S(1)}, bf16[2,224,256]{2,1,0:T(8,128)(2,1)S(1)}, u32[]{:S(2)}, u32[]{:S(2)}) collective-permute-start(bf16[2,224,256]{2,1,0:T(8,128)(2,1)S(1)} %get-tuple-element.35), channel_id=1, source_target_pairs={{0,4},{4,0},{8,12},{12,8},{16,20},{20,16},{24,28},{28,24},{1,5},{5... | collective-permute-start | bytes 688136 | tf_op jit(solution)/shard_map/ppermute | solution.py:365
  4.5 3.7 %collective-permute-start.2 = (bf16[2,32,256]{2,1,0:T(8,128)(2,1)S(1)}, bf16[2,32,256]{2,1,0:T(8,128)(2,1)S(1)}, u32[]{:S(2)}, u32[]{:S(2)}) collective-permute-start(bf16[2,32,256]{2,1,0:T(8,128)(2,1)S(1)} %get-tuple-element.38.four_ref), channel_id=1, source_target_pairs={{0,24},{4,28},{8,16},{12,20},{16,8},{20,12},{24,0},{28,4},{1,25},{... | collective-permute-start | bytes 98312 | tf_op jit(solution)/shard_map/ppermute | solution.py:365
  8.2 0.0 collective-permute-start.3
  8.2 0.8 %collective-permute-start.4 = (bf16[2,64,256]{2,1,0:T(8,128)(2,1)S(1)}, bf16[2,64,256]{2,1,0:T(8,128)(2,1)S(1)}, u32[]{:S(2)}, u32[]{:S(2)}) collective-permute-start(bf16[2,64,256]{2,1,0:T(8,128)(2,1)S(1)} %get-tuple-element.42), channel_id=1, source_target_pairs={{0,8},{4,12},{8,0},{12,4},{16,24},{20,28},{24,16},{28,20},{1,9},{5... | collective-permute-start | bytes 196616 | tf_op jit(solution)/shard_map/ppermute | solution.py:365
  9.0 0.7 %collective-permute-start.1 = (bf16[2,128,256]{2,1,0:T(8,128)(2,1)S(1)}, bf16[2,128,256]{2,1,0:T(8,128)(2,1)S(1)}, u32[]{:S(2)}, u32[]{:S(2)}) collective-permute-start(bf16[2,128,256]{2,1,0:T(8,128)(2,1)S(1)} %get-tuple-element.37), channel_id=1, source_target_pairs={{4,8},{8,4},{12,16},{16,12},{20,24},{24,20},{5,9},{9,5},{13,17},{1... | collective-permute-start | bytes 393224 | tf_op jit(solution)/shard_map/ppermute | solution.py:373
  9.6 1.0 %collective-permute-done.2.six_ref = bf16[2,32,256]{2,1,0:T(8,128)(2,1)S(1)} collective-permute-done((bf16[2,32,256]{2,1,0:T(8,128)(2,1)S(1)}, bf16[2,32,256]{2,1,0:T(8,128)(2,1)S(1)}, u32[]{:S(2)}, u32[]{:S(2)}) %collective-permute-start.2) | collective-permute-done | bytes 32800 | tf_op jit(solution)/shard_map/ppermute | solution.py:365
  10.6 2.5 %collective-permute-done.3.four_ref = bf16[2,32,256]{2,1,0:T(8,128)(2,1)S(1)} collective-permute-done((bf16[2,32,256]{2,1,0:T(8,128)(2,1)S(1)}, bf16[2,32,256]{2,1,0:T(8,128)(2,1)S(1)}, u32[]{:S(2)}, u32[]{:S(2)}) %collective-permute-start.3) | collective-permute-done | bytes 32800 | tf_op jit(solution)/shard_map/ppermute | solution.py:365
  13.1 0.0 collective-permute-done.first_ref
  13.1 0.1 relay.1
  13.2 0.0 collective-permute-done.4.three_ref
  13.3 0.6 %collective-permute-start.5 = (bf16[2,128,256]{2,1,0:T(8,128)(2,1)S(1)}, bf16[2,128,256]{2,1,0:T(8,128)(2,1)S(1)}, u32[]{:S(2)}, u32[]{:S(2)}) collective-permute-start(bf16[2,128,256]{2,1,0:T(8,128)(2,1)S(1)} %join.1.relay_a), channel_id=1, source_target_pairs={{0,4},{4,0},{8,12},{12,8},{16,20},{20,16},{24,28},{28,24},{1,5},{5... | collective-permute-start | bytes 393224 | tf_op jit(solution)/shard_map/ppermute | solution.py:365
  13.8 1.5 %local.1 = (bf16[2,128,256]{2,1,0:T(8,128)(2,1)S(1)}, bf16[128,256]{1,0:T(8,128)(2,1)S(1)}, bf16[64,256]{1,0:T(8,128)(2,1)S(1)}, bf16[32,256]{1,0:T(8,128)(2,1)S(1)}, f32[3,512,256]{2,1,0:T(8,128)S(1)}) custom-call(bf16[512,256]{1,0:T(8,128)(2,1)S(1)} %get-tuple-element.26.q_ref, bf16[512,256]{1,0:T(8,128)(2,1)S(1)} %get-tuple-element.27.k_ref, ...), custom_call_target="tpu_custom_call" | custom-call | tf_op jit(solution)/shard_map/local/pallas_call | solution.py:444
  15.4 0.0 collective-permute-done.1.second_ref
  15.4 0.0 copy-start
  15.4 1.0 %mid.1.state = f32[3,512,256]{2,1,0:T(8,128)S(1)} custom-call(bf16[2,128,256]{2,1,0:T(8,128)(2,1)S(1)} %get-tuple-element.32.edge_q, bf16[128,256]{1,0:T(8,128)(2,1)S(1)} %get-tuple-element.33.two_q, f32[3,512,256]{2,1,0:T(8,128)S(1)} %get-tuple-element.34.state, ...), custom_call_target="tpu_custom_call", output_to_operand_aliasing={{}: (2, {})} | custom-call | tf_op jit(solution)/shard_map/mid/pallas_call | solution.py:462
  16.4 1.9 %collective-permute-done.5.relay_b = bf16[2,128,256]{2,1,0:T(8,128)(2,1)S(1)} collective-permute-done((bf16[2,128,256]{2,1,0:T(8,128)(2,1)S(1)}, bf16[2,128,256]{2,1,0:T(8,128)(2,1)S(1)}, u32[]{:S(2)}, u32[]{:S(2)}) %collective-permute-start.5) | collective-permute-done | bytes 131104 | tf_op jit(solution)/shard_map/ppermute | solution.py:365
  18.3 0.6 %finish.1 = (bf16[128,256]{1,0:T(8,128)(2,1)S(1)}, bf16[128,256]{1,0:T(8,128)(2,1)S(1)}, bf16[128,256]{1,0:T(8,128)(2,1)S(1)}, bf16[128,256]{1,0:T(8,128)(2,1)S(1)}) custom-call(bf16[64,256]{1,0:T(8,128)(2,1)S(1)} %get-tuple-element.30.three_q, bf16[32,256]{1,0:T(8,128)(2,1)S(1)} %get-tuple-element.31.four_q, f32[3,512,256]{2,1,0:T(8,128)S(1)} %mid.1.state, ...), custom_call_target="tpu_custom_call" | custom-call | tf_op jit(solution)/shard_map/finish/pallas_call | solution.py:483
  18.9 0.1 collective-permute-start.6
  19.0 1.6 %collective-permute-start.7 = (bf16[128,256]{1,0:T(8,128)(2,1)S(1)}, bf16[128,256]{1,0:T(8,128)(2,1)S(1)}, u32[]{:S(2)}, u32[]{:S(2)}) collective-permute-start(bf16[128,256]{1,0:T(8,128)(2,1)S(1)} %get-tuple-element.45), channel_id=1, source_target_pairs={{0,2},{1,3},{2,0},{3,1},{4,6},{5,7},{6,4},{7,5},{8,10},{9,11},{10,... | collective-permute-start | bytes 196616 | tf_op jit(solution)/shard_map/ppermute | solution.py:365
  20.5 0.3 %collective-permute-start.8 = (bf16[128,256]{1,0:T(8,128)(2,1)S(1)}, bf16[128,256]{1,0:T(8,128)(2,1)S(1)}, u32[]{:S(2)}, u32[]{:S(2)}) collective-permute-start(bf16[128,256]{1,0:T(8,128)(2,1)S(1)} %get-tuple-element.46), channel_id=1, source_target_pairs={{0,3},{1,2},{2,1},{3,0},{4,7},{5,6},{6,5},{7,4},{8,11},{9,10},{10,... | collective-permute-start | bytes 196616 | tf_op jit(solution)/shard_map/ppermute | solution.py:365
  20.9 0.0 collective-permute-done.6.next_ref
  20.9 0.0 copy-done
  20.9 0.3 %partial.1.partial_ref = f32[128,1024]{1,0:T(8,128)S(1)} custom-call(bf16[128,256]{1,0:T(8,128)(2,1)S(1)} %get-tuple-element.43.near_ref, bf16[128,256]{1,0:T(8,128)(2,1)S(1)} %collective-permute-done.6.next_ref, bf16[1024,1024]{1,0:T(8,128)(2,1)S(1)} %copy-done), custom_call_target="tpu_custom_call" | custom-call | tf_op jit(solution)/shard_map/partial/pallas_call | solution.py:497
  21.2 2.3 %collective-permute-done.7.refs_0_ = bf16[128,256]{1,0:T(8,128)(2,1)S(1)} collective-permute-done((bf16[128,256]{1,0:T(8,128)(2,1)S(1)}, bf16[128,256]{1,0:T(8,128)(2,1)S(1)}, u32[]{:S(2)}, u32[]{:S(2)}) %collective-permute-start.7) | collective-permute-done | bytes 65568 | tf_op jit(solution)/shard_map/ppermute | solution.py:365
  23.5 1.1 %collective-permute-done.8.refs_1_ = bf16[128,256]{1,0:T(8,128)(2,1)S(1)} collective-permute-done((bf16[128,256]{1,0:T(8,128)(2,1)S(1)}, bf16[128,256]{1,0:T(8,128)(2,1)S(1)}, u32[]{:S(2)}, u32[]{:S(2)}) %collective-permute-start.8) | collective-permute-done | bytes 65568 | tf_op jit(solution)/shard_map/ppermute | solution.py:365
  24.6 1.0 %project.1 = bf16[128,1024]{1,0:T(8,128)(2,1)} custom-call(f32[128,1024]{1,0:T(8,128)S(1)} %partial.1.partial_ref, bf16[128,256]{1,0:T(8,128)(2,1)S(1)} %collective-permute-done.7.refs_0_, bf16[128,256]{1,0:T(8,128)(2,1)S(1)} %collective-permute-done.8.refs_1_, bf16[1024,1024]{1,0:T(8,128)(2,1)S(1)} %copy-done), custom_call_target="tpu_custom_call" | custom-call | tf_op jit(solution)/shard_map/project/pallas_call | solution.py:504
  (2 shorter events, 0.1 us)
Async XLA Ops:
  1.4 11.7 %collective-permute-start = (bf16[2,224,256]{2,1,0:T(8,128)(2,1)S(1)}, bf16[2,224,256]{2,1,0:T(8,128)(2,1)S(1)}, u32[]{:S(2)}, u32[]{:S(2)}) collective-permute-start(bf16[2,224,256]{2,1,0:T(8,128)(2,1)S(1)} %get-tuple-element.35), channel_id=1, source_target_pairs={{0,4},{4,0},{8,12},{12,8},{16,20},{20,16},{24,28},{28,24},{1,5},{5... | collective-permute-start | bytes 688136 | tf_op jit(solution)/shard_map/ppermute | solution.py:365
  4.5 6.1 %collective-permute-start.2 = (bf16[2,32,256]{2,1,0:T(8,128)(2,1)S(1)}, bf16[2,32,256]{2,1,0:T(8,128)(2,1)S(1)}, u32[]{:S(2)}, u32[]{:S(2)}) collective-permute-start(bf16[2,32,256]{2,1,0:T(8,128)(2,1)S(1)} %get-tuple-element.38.four_ref), channel_id=1, source_target_pairs={{0,24},{4,28},{8,16},{12,20},{16,8},{20,12},{24,0},{28,4},{1,25},{... | collective-permute-start | bytes 98312 | tf_op jit(solution)/shard_map/ppermute | solution.py:365
  8.2 4.9 %collective-permute-start.3 = (bf16[2,32,256]{2,1,0:T(8,128)(2,1)S(1)}, bf16[2,32,256]{2,1,0:T(8,128)(2,1)S(1)}, u32[]{:S(2)}, u32[]{:S(2)}) collective-permute-start(bf16[2,32,256]{2,1,0:T(8,128)(2,1)S(1)} %get-tuple-element.38.four_ref), channel_id=1, source_target_pairs={{0,16},{4,20},{8,24},{12,28},{16,0},{20,4},{24,8},{28,12},{1,17},{... | collective-permute-start | bytes 98312 | tf_op jit(solution)/shard_map/ppermute | solution.py:365
  8.2 5.1 %collective-permute-start.4 = (bf16[2,64,256]{2,1,0:T(8,128)(2,1)S(1)}, bf16[2,64,256]{2,1,0:T(8,128)(2,1)S(1)}, u32[]{:S(2)}, u32[]{:S(2)}) collective-permute-start(bf16[2,64,256]{2,1,0:T(8,128)(2,1)S(1)} %get-tuple-element.42), channel_id=1, source_target_pairs={{0,8},{4,12},{8,0},{12,4},{16,24},{20,28},{24,16},{28,20},{1,9},{5... | collective-permute-start | bytes 196616 | tf_op jit(solution)/shard_map/ppermute | solution.py:365
  9.0 6.4 %collective-permute-start.1 = (bf16[2,128,256]{2,1,0:T(8,128)(2,1)S(1)}, bf16[2,128,256]{2,1,0:T(8,128)(2,1)S(1)}, u32[]{:S(2)}, u32[]{:S(2)}) collective-permute-start(bf16[2,128,256]{2,1,0:T(8,128)(2,1)S(1)} %get-tuple-element.37), channel_id=1, source_target_pairs={{4,8},{8,4},{12,16},{16,12},{20,24},{24,20},{5,9},{9,5},{13,17},{1... | collective-permute-start | bytes 393224 | tf_op jit(solution)/shard_map/ppermute | solution.py:373
  13.3 5.0 %collective-permute-start.5 = (bf16[2,128,256]{2,1,0:T(8,128)(2,1)S(1)}, bf16[2,128,256]{2,1,0:T(8,128)(2,1)S(1)}, u32[]{:S(2)}, u32[]{:S(2)}) collective-permute-start(bf16[2,128,256]{2,1,0:T(8,128)(2,1)S(1)} %join.1.relay_a), channel_id=1, source_target_pairs={{0,4},{4,0},{8,12},{12,8},{16,20},{20,16},{24,28},{28,24},{1,5},{5... | collective-permute-start | bytes 393224 | tf_op jit(solution)/shard_map/ppermute | solution.py:365
  15.4 5.5 %copy-start = (bf16[1024,1024]{1,0:T(8,128)(2,1)S(1)}, bf16[1024,1024]{1,0:T(8,128)(2,1)}, u32[]{:S(2)}) copy-start(bf16[1024,1024]{1,0:T(8,128)(2,1)} %refs_2_.1) | copy-start | bytes 6291460
  18.9 1.9 %collective-permute-start.6 = (bf16[128,256]{1,0:T(8,128)(2,1)S(1)}, bf16[128,256]{1,0:T(8,128)(2,1)S(1)}, u32[]{:S(2)}, u32[]{:S(2)}) collective-permute-start(bf16[128,256]{1,0:T(8,128)(2,1)S(1)} %get-tuple-element.44), channel_id=1, source_target_pairs={{0,1},{1,0},{2,3},{3,2},{4,5},{5,4},{6,7},{7,6},{8,9},{9,8},{10,11... | collective-permute-start | bytes 196616 | tf_op jit(solution)/shard_map/ppermute | solution.py:365
  19.0 4.5 %collective-permute-start.7 = (bf16[128,256]{1,0:T(8,128)(2,1)S(1)}, bf16[128,256]{1,0:T(8,128)(2,1)S(1)}, u32[]{:S(2)}, u32[]{:S(2)}) collective-permute-start(bf16[128,256]{1,0:T(8,128)(2,1)S(1)} %get-tuple-element.45), channel_id=1, source_target_pairs={{0,2},{1,3},{2,0},{3,1},{4,6},{5,7},{6,4},{7,5},{8,10},{9,11},{10,... | collective-permute-start | bytes 196616 | tf_op jit(solution)/shard_map/ppermute | solution.py:365
  20.5 4.0 %collective-permute-start.8 = (bf16[128,256]{1,0:T(8,128)(2,1)S(1)}, bf16[128,256]{1,0:T(8,128)(2,1)S(1)}, u32[]{:S(2)}, u32[]{:S(2)}) collective-permute-start(bf16[128,256]{1,0:T(8,128)(2,1)S(1)} %get-tuple-element.46), channel_id=1, source_target_pairs={{0,3},{1,2},{2,1},{3,0},{4,7},{5,6},{6,5},{7,4},{8,11},{9,10},{10,... | collective-permute-start | bytes 196616 | tf_op jit(solution)/shard_map/ppermute | solution.py:365
where the time goes:
time: 25.8 us; the launch traced here: 25.6 us
  starting transfers between devices  10.6 us (41%)
  waiting for transfers between devices  8.78 us (34%)
  Pallas kernels  6.1 us (24%)
    ppermute x8, starting transfers between devices, swapped(): lax.ppermute(block, axis, [(i, i ^ mask) for i in range(lax.axis_size(axi...  9.99 us
    ppermute x8, waiting for transfers between devices, swapped(): lax.ppermute(block, axis, [(i, i ^ mask) for i in range(lax.axis_size(axi...  8.78 us
    pallas_call x1, Pallas kernels, per_device(): pl.pallas_call(local_kernel, out_shape=[bf16(2, BLOCK, features), bf16(ro...  1.54 us
    pallas_call x1, Pallas kernels, per_device(): pl.pallas_call(pool_kernel, in_specs=[hbm] * 3, out_shape=[bf16(rows, fea...  1.42 us
    pallas_call x1, Pallas kernels, per_device(): pl.pallas_call(project_kernel, in_specs=[vmem] * len(parts), out_specs=hb...  1.04 us
    pallas_call x1, Pallas kernels, per_device(): pl.pallas_call(mid_kernel, out_shape=jax.ShapeDtypeStruct((3, rows, featu...  1 us
    ppermute x1, starting transfers between devices, across(): return lax.ppermute(block, axis, route)  0.66 us
    pallas_call x1, Pallas kernels, per_device(): pl.pallas_call(finish_kernel, out_shape=[bf16(BLOCK, features) for _ in r...  0.62 us
  transfers between devices with their start and end apart: 9, of which 5 were waited for; matrix products, arithmetic and copies ran while one was open for 0% of the time, Pallas kernels for 12%

commit v1 on v0

--- a/solution.py
+++ b/solution.py
@@ -365,12 +365,15 @@
     return lax.ppermute(block, axis, [(i, i ^ mask) for i in range(lax.axis_size(axis))])
 
 
-def across(block, axis):
-    count = lax.axis_size(axis)
+def across(block):
+    count, heads = lax.axis_size("seq"), lax.axis_size("head")
     route = []
-    for low in range(1, count - 1, 2):
-        route += [(low, low + 1), (low + 1, low)]
-    return lax.ppermute(block, axis, route)
+    for seq in range(count):
+        end = seq in (0, count - 1)
+        other = seq if end else seq + 1 if seq % 2 else seq - 1
+        for head in range(heads):
+            route.append((seq * heads + head, other * heads + (head ^ 1 if end else head)))
+    return lax.ppermute(block, ("seq", "head"), route)
 
 
 def per_device(queries, key_vectors, value_vectors, out_weight):
@@ -418,7 +421,7 @@
     )(keys, values, two)
 
     first_in = swapped(first, "seq", 1)
-    second_in = across(second, "seq")
+    second_in = across(second)
     fours_in = [swapped(four, "seq", mask) for mask in (6, 4)]
     three_in = swapped(three, "seq", 2)
     pack, two_in, near = pl.pallas_call(

time: 25.8 us -> 26.1 us (1.012)
  waiting for transfers between devices: 8.78 us -> 10.2 us
  starting transfers between devices: 10.6 us -> 9.57 us
    ppermute x8, waiting for transfers between devices: 8.78 us -> 10.2 us  [swapped(): lax.ppermute(block, axis, [(i, i ^ mask) for i in range(lax.axis_size(axi...]
    ppermute x1, starting transfers between devices: 0.66 us -> 0.01 us  [across(): return lax.ppermute(block, ('seq', 'head'), route)]
    ppermute x8, starting transfers between devices: 9.99 us -> 9.57 us  [swapped(): lax.ppermute(block, axis, [(i, i ^ mask) for i in range(lax.axis_size(axi...]
where the time goes in v1:
time: 26.1 us; the launch traced here: 25.9 us
  waiting for transfers between devices  10.2 us (39%)
  starting transfers between devices  9.57 us (37%)
  Pallas kernels  6.1 us (23%)
    ppermute x8, waiting for transfers between devices, swapped(): lax.ppermute(block, axis, [(i, i ^ mask) for i in range(lax.axis_size(axi...  10.2 us
    ppermute x8, starting transfers between devices, swapped(): lax.ppermute(block, axis, [(i, i ^ mask) for i in range(lax.axis_size(axi...  9.57 us
    pallas_call x1, Pallas kernels, per_device(): pl.pallas_call(local_kernel, out_shape=[bf16(2, BLOCK, features), bf16(ro...  1.54 us
    pallas_call x1, Pallas kernels, per_device(): pl.pallas_call(pool_kernel, in_specs=[hbm] * 3, out_shape=[bf16(rows, fea...  1.42 us
    pallas_call x1, Pallas kernels, per_device(): pl.pallas_call(project_kernel, in_specs=[vmem] * len(parts), out_specs=hb...  1.04 us
    pallas_call x1, Pallas kernels, per_device(): pl.pallas_call(mid_kernel, out_shape=jax.ShapeDtypeStruct((3, rows, featu...  0.99 us
    pallas_call x1, Pallas kernels, per_device(): pl.pallas_call(finish_kernel, out_shape=[bf16(BLOCK, features) for _ in r...  0.62 us
  transfers between devices with their start and end apart: 9, of which 5 were waited for; matrix products, arithmetic and copies ran while one was open for 0% of the time, Pallas kernels for 12%

profile of v1, /device:TPU:0, one launch (start us, length us, event | category | flops | bytes accessed | tf_op | source)
XLA Modules:
  0.0 25.9 jit_solution(16046792411760209549)
XLA Ops:
  0.0 1.4 %pool.1 = (bf16[512,256]{1,0:T(8,128)(2,1)S(1)}, bf16[512,256]{1,0:T(8,128)(2,1)S(1)}, bf16[512,256]{1,0:T(8,128)(2,1)S(1)}, bf16[2,224,256]{2,1,0:T(8,128)(2,1)...) custom-call(bf16[1,512,256]{2,1,0:T(8,128)(2,1)} %k_hbm.1, bf16[1,512,256]{2,1,0:T(8,128)(2,1)} %v_hbm.1, ...), custom_call_target="tpu_custom_call" | custom-call | tf_op jit(solution)/shard_map/pool/pallas_call | solution.py:392
  1.4 3.0 %collective-permute-start = (bf16[2,224,256]{2,1,0:T(8,128)(2,1)S(1)}, bf16[2,224,256]{2,1,0:T(8,128)(2,1)S(1)}, u32[]{:S(2)}, u32[]{:S(2)}) collective-permute-start(bf16[2,224,256]{2,1,0:T(8,128)(2,1)S(1)} %get-tuple-element.35), channel_id=1, source_target_pairs={{0,4},{4,0},{8,12},{12,8},{16,20},{20,16},{24,28},{28,24},{1,5},{5... | collective-permute-start | bytes 688136 | tf_op jit(solution)/shard_map/ppermute | solution.py:365
  4.5 3.7 %collective-permute-start.2 = (bf16[2,32,256]{2,1,0:T(8,128)(2,1)S(1)}, bf16[2,32,256]{2,1,0:T(8,128)(2,1)S(1)}, u32[]{:S(2)}, u32[]{:S(2)}) collective-permute-start(bf16[2,32,256]{2,1,0:T(8,128)(2,1)S(1)} %get-tuple-element.38.four_ref), channel_id=1, source_target_pairs={{0,24},{4,28},{8,16},{12,20},{16,8},{20,12},{24,0},{28,4},{1,25},{... | collective-permute-start | bytes 98312 | tf_op jit(solution)/shard_map/ppermute | solution.py:365
  8.2 0.0 collective-permute-start.3
  8.2 0.8 %collective-permute-start.4 = (bf16[2,64,256]{2,1,0:T(8,128)(2,1)S(1)}, bf16[2,64,256]{2,1,0:T(8,128)(2,1)S(1)}, u32[]{:S(2)}, u32[]{:S(2)}) collective-permute-start(bf16[2,64,256]{2,1,0:T(8,128)(2,1)S(1)} %get-tuple-element.42), channel_id=1, source_target_pairs={{0,8},{4,12},{8,0},{12,4},{16,24},{20,28},{24,16},{28,20},{1,9},{5... | collective-permute-start | bytes 196616 | tf_op jit(solution)/shard_map/ppermute | solution.py:365
  9.0 0.0 collective-permute-start.1
  9.0 1.7 %collective-permute-done.2.six_ref = bf16[2,32,256]{2,1,0:T(8,128)(2,1)S(1)} collective-permute-done((bf16[2,32,256]{2,1,0:T(8,128)(2,1)S(1)}, bf16[2,32,256]{2,1,0:T(8,128)(2,1)S(1)}, u32[]{:S(2)}, u32[]{:S(2)}) %collective-permute-start.2) | collective-permute-done | bytes 32800 | tf_op jit(solution)/shard_map/ppermute | solution.py:365
  10.6 2.8 %collective-permute-done.3.four_ref = bf16[2,32,256]{2,1,0:T(8,128)(2,1)S(1)} collective-permute-done((bf16[2,32,256]{2,1,0:T(8,128)(2,1)S(1)}, bf16[2,32,256]{2,1,0:T(8,128)(2,1)S(1)}, u32[]{:S(2)}, u32[]{:S(2)}) %collective-permute-start.3) | collective-permute-done | bytes 32800 | tf_op jit(solution)/shard_map/ppermute | solution.py:365
  13.4 0.0 collective-permute-done.first_ref
  13.4 0.1 relay.1
  13.5 0.0 collective-permute-done.4.three_ref
  13.6 0.2 collective-permute-start.5
  13.7 1.5 %local.1 = (bf16[2,128,256]{2,1,0:T(8,128)(2,1)S(1)}, bf16[128,256]{1,0:T(8,128)(2,1)S(1)}, bf16[64,256]{1,0:T(8,128)(2,1)S(1)}, bf16[32,256]{1,0:T(8,128)(2,1)S(1)}, f32[3,512,256]{2,1,0:T(8,128)S(1)}) custom-call(bf16[512,256]{1,0:T(8,128)(2,1)S(1)} %get-tuple-element.26.q_ref, bf16[512,256]{1,0:T(8,128)(2,1)S(1)} %get-tuple-element.27.k_ref, ...), custom_call_target="tpu_custom_call" | custom-call | tf_op jit(solution)/shard_map/local/pallas_call | solution.py:447
  15.3 0.0 collective-permute-done.1.second_ref
  15.3 0.0 copy-start
  15.3 1.0 %mid.1.state = f32[3,512,256]{2,1,0:T(8,128)S(1)} custom-call(bf16[2,128,256]{2,1,0:T(8,128)(2,1)S(1)} %get-tuple-element.32.edge_q, bf16[128,256]{1,0:T(8,128)(2,1)S(1)} %get-tuple-element.33.two_q, f32[3,512,256]{2,1,0:T(8,128)S(1)} %get-tuple-element.34.state, ...), custom_call_target="tpu_custom_call", output_to_operand_aliasing={{}: (2, {})} | custom-call | tf_op jit(solution)/shard_map/mid/pallas_call | solution.py:465
  16.3 2.3 %collective-permute-done.5.relay_b = bf16[2,128,256]{2,1,0:T(8,128)(2,1)S(1)} collective-permute-done((bf16[2,128,256]{2,1,0:T(8,128)(2,1)S(1)}, bf16[2,128,256]{2,1,0:T(8,128)(2,1)S(1)}, u32[]{:S(2)}, u32[]{:S(2)}) %collective-permute-start.5) | collective-permute-done | bytes 131104 | tf_op jit(solution)/shard_map/ppermute | solution.py:365
  18.6 0.6 %finish.1 = (bf16[128,256]{1,0:T(8,128)(2,1)S(1)}, bf16[128,256]{1,0:T(8,128)(2,1)S(1)}, bf16[128,256]{1,0:T(8,128)(2,1)S(1)}, bf16[128,256]{1,0:T(8,128)(2,1)S(1)}) custom-call(bf16[64,256]{1,0:T(8,128)(2,1)S(1)} %get-tuple-element.30.three_q, bf16[32,256]{1,0:T(8,128)(2,1)S(1)} %get-tuple-element.31.four_q, f32[3,512,256]{2,1,0:T(8,128)S(1)} %mid.1.state, ...), custom_call_target="tpu_custom_call" | custom-call | tf_op jit(solution)/shard_map/finish/pallas_call | solution.py:486
  19.2 0.1 collective-permute-start.6
  19.3 1.6 %collective-permute-start.7 = (bf16[128,256]{1,0:T(8,128)(2,1)S(1)}, bf16[128,256]{1,0:T(8,128)(2,1)S(1)}, u32[]{:S(2)}, u32[]{:S(2)}) collective-permute-start(bf16[128,256]{1,0:T(8,128)(2,1)S(1)} %get-tuple-element.45), channel_id=1, source_target_pairs={{0,2},{1,3},{2,0},{3,1},{4,6},{5,7},{6,4},{7,5},{8,10},{9,11},{10,... | collective-permute-start | bytes 196616 | tf_op jit(solution)/shard_map/ppermute | solution.py:365
  20.9 0.3 %collective-permute-start.8 = (bf16[128,256]{1,0:T(8,128)(2,1)S(1)}, bf16[128,256]{1,0:T(8,128)(2,1)S(1)}, u32[]{:S(2)}, u32[]{:S(2)}) collective-permute-start(bf16[128,256]{1,0:T(8,128)(2,1)S(1)} %get-tuple-element.46), channel_id=1, source_target_pairs={{0,3},{1,2},{2,1},{3,0},{4,7},{5,6},{6,5},{7,4},{8,11},{9,10},{10,... | collective-permute-start | bytes 196616 | tf_op jit(solution)/shard_map/ppermute | solution.py:365
  21.2 0.0 collective-permute-done.6.next_ref
  21.2 0.0 copy-done
  21.2 0.3 %partial.1.partial_ref = f32[128,1024]{1,0:T(8,128)S(1)} custom-call(bf16[128,256]{1,0:T(8,128)(2,1)S(1)} %get-tuple-element.43.near_ref, bf16[128,256]{1,0:T(8,128)(2,1)S(1)} %collective-permute-done.6.next_ref, bf16[1024,1024]{1,0:T(8,128)(2,1)S(1)} %copy-done), custom_call_target="tpu_custom_call" | custom-call | tf_op jit(solution)/shard_map/partial/pallas_call | solution.py:500
  21.5 2.3 %collective-permute-done.7.refs_0_ = bf16[128,256]{1,0:T(8,128)(2,1)S(1)} collective-permute-done((bf16[128,256]{1,0:T(8,128)(2,1)S(1)}, bf16[128,256]{1,0:T(8,128)(2,1)S(1)}, u32[]{:S(2)}, u32[]{:S(2)}) %collective-permute-start.7) | collective-permute-done | bytes 65568 | tf_op jit(solution)/shard_map/ppermute | solution.py:365
  23.8 1.1 %collective-permute-done.8.refs_1_ = bf16[128,256]{1,0:T(8,128)(2,1)S(1)} collective-permute-done((bf16[128,256]{1,0:T(8,128)(2,1)S(1)}, bf16[128,256]{1,0:T(8,128)(2,1)S(1)}, u32[]{:S(2)}, u32[]{:S(2)}) %collective-permute-start.8) | collective-permute-done | bytes 65568 | tf_op jit(solution)/shard_map/ppermute | solution.py:365
  24.9 1.0 %project.1 = bf16[128,1024]{1,0:T(8,128)(2,1)} custom-call(f32[128,1024]{1,0:T(8,128)S(1)} %partial.1.partial_ref, bf16[128,256]{1,0:T(8,128)(2,1)S(1)} %collective-permute-done.7.refs_0_, bf16[128,256]{1,0:T(8,128)(2,1)S(1)} %collective-permute-done.8.refs_1_, bf16[1024,1024]{1,0:T(8,128)(2,1)S(1)} %copy-done), custom_call_target="tpu_custom_call" | custom-call | tf_op jit(solution)/shard_map/project/pallas_call | solution.py:507
  (2 shorter events, 0.1 us)
Async XLA Ops:
  1.4 12.0 %collective-permute-start = (bf16[2,224,256]{2,1,0:T(8,128)(2,1)S(1)}, bf16[2,224,256]{2,1,0:T(8,128)(2,1)S(1)}, u32[]{:S(2)}, u32[]{:S(2)}) collective-permute-start(bf16[2,224,256]{2,1,0:T(8,128)(2,1)S(1)} %get-tuple-element.35), channel_id=1, source_target_pairs={{0,4},{4,0},{8,12},{12,8},{16,20},{20,16},{24,28},{28,24},{1,5},{5... | collective-permute-start | bytes 688136 | tf_op jit(solution)/shard_map/ppermute | solution.py:365
  4.5 6.1 %collective-permute-start.2 = (bf16[2,32,256]{2,1,0:T(8,128)(2,1)S(1)}, bf16[2,32,256]{2,1,0:T(8,128)(2,1)S(1)}, u32[]{:S(2)}, u32[]{:S(2)}) collective-permute-start(bf16[2,32,256]{2,1,0:T(8,128)(2,1)S(1)} %get-tuple-element.38.four_ref), channel_id=1, source_target_pairs={{0,24},{4,28},{8,16},{12,20},{16,8},{20,12},{24,0},{28,4},{1,25},{... | collective-permute-start | bytes 98312 | tf_op jit(solution)/shard_map/ppermute | solution.py:365
  8.2 5.2 %collective-permute-start.3 = (bf16[2,32,256]{2,1,0:T(8,128)(2,1)S(1)}, bf16[2,32,256]{2,1,0:T(8,128)(2,1)S(1)}, u32[]{:S(2)}, u32[]{:S(2)}) collective-permute-start(bf16[2,32,256]{2,1,0:T(8,128)(2,1)S(1)} %get-tuple-element.38.four_ref), channel_id=1, source_target_pairs={{0,16},{4,20},{8,24},{12,28},{16,0},{20,4},{24,8},{28,12},{1,17},{... | collective-permute-start | bytes 98312 | tf_op jit(solution)/shard_map/ppermute | solution.py:365
  8.2 5.4 %collective-permute-start.4 = (bf16[2,64,256]{2,1,0:T(8,128)(2,1)S(1)}, bf16[2,64,256]{2,1,0:T(8,128)(2,1)S(1)}, u32[]{:S(2)}, u32[]{:S(2)}) collective-permute-start(bf16[2,64,256]{2,1,0:T(8,128)(2,1)S(1)} %get-tuple-element.42), channel_id=1, source_target_pairs={{0,8},{4,12},{8,0},{12,4},{16,24},{20,28},{24,16},{28,20},{1,9},{5... | collective-permute-start | bytes 196616 | tf_op jit(solution)/shard_map/ppermute | solution.py:365
  9.0 6.3 %collective-permute-start.1 = (bf16[2,128,256]{2,1,0:T(8,128)(2,1)S(1)}, bf16[2,128,256]{2,1,0:T(8,128)(2,1)S(1)}, u32[]{:S(2)}, u32[]{:S(2)}) collective-permute-start(bf16[2,128,256]{2,1,0:T(8,128)(2,1)S(1)} %get-tuple-element.37), channel_id=1, source_target_pairs={{0,1},{1,0},{2,3},{3,2},{4,8},{5,9},{6,10},{7,11},{8,4},{9,5},{10,... | collective-permute-start | bytes 393224 | tf_op jit(solution)/shard_map/ppermute | solution.py:376
  13.6 5.0 %collective-permute-start.5 = (bf16[2,128,256]{2,1,0:T(8,128)(2,1)S(1)}, bf16[2,128,256]{2,1,0:T(8,128)(2,1)S(1)}, u32[]{:S(2)}, u32[]{:S(2)}) collective-permute-start(bf16[2,128,256]{2,1,0:T(8,128)(2,1)S(1)} %join.1.relay_a), channel_id=1, source_target_pairs={{0,4},{4,0},{8,12},{12,8},{16,20},{20,16},{24,28},{28,24},{1,5},{5... | collective-permute-start | bytes 393224 | tf_op jit(solution)/shard_map/ppermute | solution.py:365
  15.3 5.9 %copy-start = (bf16[1024,1024]{1,0:T(8,128)(2,1)S(1)}, bf16[1024,1024]{1,0:T(8,128)(2,1)}, u32[]{:S(2)}) copy-start(bf16[1024,1024]{1,0:T(8,128)(2,1)} %refs_2_.1) | copy-start | bytes 6291460
  19.2 1.9 %collective-permute-start.6 = (bf16[128,256]{1,0:T(8,128)(2,1)S(1)}, bf16[128,256]{1,0:T(8,128)(2,1)S(1)}, u32[]{:S(2)}, u32[]{:S(2)}) collective-permute-start(bf16[128,256]{1,0:T(8,128)(2,1)S(1)} %get-tuple-element.44), channel_id=1, source_target_pairs={{0,1},{1,0},{2,3},{3,2},{4,5},{5,4},{6,7},{7,6},{8,9},{9,8},{10,11... | collective-permute-start | bytes 196616 | tf_op jit(solution)/shard_map/ppermute | solution.py:365
  19.3 4.5 %collective-permute-start.7 = (bf16[128,256]{1,0:T(8,128)(2,1)S(1)}, bf16[128,256]{1,0:T(8,128)(2,1)S(1)}, u32[]{:S(2)}, u32[]{:S(2)}) collective-permute-start(bf16[128,256]{1,0:T(8,128)(2,1)S(1)} %get-tuple-element.45), channel_id=1, source_target_pairs={{0,2},{1,3},{2,0},{3,1},{4,6},{5,7},{6,4},{7,5},{8,10},{9,11},{10,... | collective-permute-start | bytes 196616 | tf_op jit(solution)/shard_map/ppermute | solution.py:365
  20.9 4.0 %collective-permute-start.8 = (bf16[128,256]{1,0:T(8,128)(2,1)S(1)}, bf16[128,256]{1,0:T(8,128)(2,1)S(1)}, u32[]{:S(2)}, u32[]{:S(2)}) collective-permute-start(bf16[128,256]{1,0:T(8,128)(2,1)S(1)} %get-tuple-element.46), channel_id=1, source_target_pairs={{0,3},{1,2},{2,1},{3,0},{4,7},{5,6},{6,5},{7,4},{8,11},{9,10},{10,... | collective-permute-start | bytes 196616 | tf_op jit(solution)/shard_map/ppermute | solution.py:365
